TPU v7x, 256 devices: a whole 4x4x8 slice. The times are simulated.
256 devices in a mesh: gx: 8 (over z_hi, core), gy: 4 (over y), gz: 8 (over x, z_lo).
Axes of the slice: x: 4, y: 4, z: 8 (z_hi: 4, z_lo: 2; z = z_hi * 2 + z_lo), core: 2. Of those that a mesh axis runs over, the one named last changes fastest.
Arguments:
- latent: bfloat16 [64, 64, 128, 256], P('gx', 'gy', 'gz'), may hold values from -700 to 700
- norm_gain: float32 [256], replicated, may hold values from 0.5 to 1.5
- norm_shift: float32 [256], replicated, may hold values from -3 to 3
- w_qkv: bfloat16 [256, 768], replicated, may hold values from -40 to 40
- w_out: bfloat16 [256, 256], replicated, may hold values from -0.375 to 0.375
- b_out: float32 [256], replicated, may hold values from -3 to 3
- depth_limit: int32 [16, 16, 32], P('gx', 'gy', 'gz'), may hold values from 0 to 1
Outputs:
- attended_out: bfloat16 [64, 64, 128, 256], P('gx', 'gy', 'gz')
All inputs are finite; a program needn't handle non-finite values.
Results may differ from a plain program's by a relative error of at most 0.038.
Values may be sent and summed in bfloat16 or wider, within the bound.
No kernel may reach another device: no remote copies, remote signals or barrier semaphores. Data moves between devices by JAX's collectives and lax.ppermute only.
A program may use at most 128 MiB of HBM per device.

v0:
```python
import functools

import jax
import jax.numpy as jnp
import numpy as np
from jax import lax
from jax.experimental import pallas as pl
from jax.experimental.pallas import tpu as pltpu
from jax.sharding import PartitionSpec as P

GROUPS = 32
AXES = ("gx", "gy", "gz")
f32, bf = jnp.float32, jnp.bfloat16
NT = (((1,), (1,)), ((), ()))
SCALE = float(np.log2(np.e) / np.sqrt(32.0))
VMEM = pl.BlockSpec(memory_space=pltpu.VMEM)
SMEM = pl.BlockSpec(memory_space=pltpu.SMEM)
HBM = pl.BlockSpec(memory_space=pl.ANY)


def iota(shape, dim):
    return lax.broadcasted_iota(jnp.int32, shape, dim)


def exact_dot(a, b):
    return jnp.dot(a, b, precision=lax.Precision.HIGHEST, preferred_element_type=f32)


def low_rows(a, b):
    return jnp.where(iota(a.shape, 0) < 4, a, pltpu.roll(b, 4, 0))


def high_rows(a, b):
    return jnp.where(iota(a.shape, 0) < 4, pltpu.roll(a, 4, 0), b)


def block_rows(x_ref, x, y, half):
    lows, highs = [], []
    for pair in range(2):
        a, b = [x_ref[x, y + pair * 2 + k, half * 8 : half * 8 + 8].astype(f32) for k in range(2)]
        lows.append(low_rows(a, b))
        highs.append(high_rows(a, b))
    return [jnp.concatenate(parts, axis=0).astype(bf) for parts in (lows, highs)]


def z_faces_kernel(x_ref, low_ref, high_ref):
    for bx in range(2):
        for by in range(4):
            for x in range(4):
                rows = slice(x * 16, x * 16 + 16)
                low_ref[bx, by, rows] = block_rows(x_ref, bx * 4 + x, by * 4, 0)[0]
                high_ref[bx, by, rows] = block_rows(x_ref, bx * 4 + x, by * 4, 1)[1]


def z_faces(latent):
    face = jax.ShapeDtypeStruct((2, 4, 64, 256), bf)
    return pl.pallas_call(
        z_faces_kernel,
        out_shape=[face, face],
        in_specs=[VMEM],
        out_specs=[VMEM] * 2,
        compiler_params=pltpu.CompilerParams(vmem_limit_bytes=16 * 2**20),
    )(latent)


def arrange_kernel(x_ref, own0_ref, own1_ref, row_ref):
    for bx, own_ref in enumerate((own0_ref, own1_ref)):
        for by in range(4):
            for x in range(4):
                for half in range(2):
                    for k, piece in enumerate(block_rows(x_ref, bx * 4 + x, by * 4, half)):
                        own_ref[by, half * 2 + k, x * 16 : x * 16 + 16] = piece
    entries = 2048 * 8

    def sums(i, acc):
        return acc + jnp.sum(x_ref[i].astype(f32).reshape(32, 8, 256), axis=0)

    zeros = jnp.zeros((8, 256), f32)
    total = lax.fori_loop(0, 8, sums, zeros)
    total = jnp.broadcast_to(jnp.sum(total, axis=0, keepdims=True), (8, 256)) * (1.0 / entries)
    same = (iota((256, 256), 0) // 8 == iota((256, 256), 1) // 8).astype(f32)
    mean = exact_dot(total, same)

    def squares(i, acc):
        cells = x_ref[i].astype(f32) - mean[:1][None]
        return acc + jnp.sum((cells * cells).reshape(32, 8, 256), axis=0)

    acc = lax.fori_loop(0, 8, squares, zeros)
    acc = jnp.broadcast_to(jnp.sum(acc, axis=0, keepdims=True), (8, 256))
    first = (iota((256, 128), 0) // 8 == iota((256, 128), 1)).astype(f32)
    second = (iota((256, 128), 0) // 8 + 32 == iota((256, 128), 1)).astype(f32)
    row = exact_dot(total, first) + exact_dot(acc, second)
    row_ref[...] = jnp.broadcast_to(row[:1], row_ref.shape)


def arrange(latent):
    own = jax.ShapeDtypeStruct((4, 4, 64, 256), bf)
    return pl.pallas_call(
        arrange_kernel,
        out_shape=[own, own, jax.ShapeDtypeStruct((8, 128), f32)],
        in_specs=[VMEM],
        out_specs=[VMEM] * 3,
        compiler_params=pltpu.CompilerParams(vmem_limit_bytes=16 * 2**20),
    )(latent)


def edges_kernel(entries, held_ref, zlow, zhigh, low_ref, high_ref, rows_ref):
    for x, out in enumerate((low_ref, high_ref)):
        out[0], out[1] = zlow[x], zhigh[x]
    held = held_ref[...]
    share = 1.0 / held.shape[0]
    total = jnp.sum(held, axis=0, keepdims=True)
    apart = held - total * share
    spread = jnp.sum(apart * apart, axis=0, keepdims=True) * (entries / 8)
    total, spread = jnp.broadcast_to(total, (8, 128)), jnp.broadcast_to(spread, (8, 128))
    lane = iota((8, 128), 1)
    merged = jnp.where(lane < 64, total * (1.0 / 8) + pltpu.roll(spread, 32, 1), 0.0)
    merged = jnp.where(lane < 32, total * share, merged)
    rows_ref[...] = jnp.broadcast_to(merged[:1], rows_ref.shape)


def y_faces_kernel(own0, own1, zlow, zhigh, xlow, xhigh, xzlow, xzhigh, low_ref, high_ref):
    for y, out in ((0, low_ref), (3, high_ref)):
        for x, (inner, zhalo) in enumerate(((xlow, xzlow), (own0, None), (own1, None), (xhigh, xzhigh))):
            out[x, 1:5] = inner[y]
            out[x, 0] = zlow[x - 1, y] if zhalo is None else zhalo[0, y]
            out[x, 5] = zhigh[x - 1, y] if zhalo is None else zhalo[1, y]


def faces(kernel, shape, parts, *more):
    face = jax.ShapeDtypeStruct(shape, bf)
    return pl.pallas_call(
        kernel,
        out_shape=[face, face, *more],
        in_specs=[VMEM] * len(parts),
        out_specs=[VMEM] * (2 + len(more)),
        compiler_params=pltpu.CompilerParams(vmem_limit_bytes=16 * 2**20),
    )(*parts)


def interleave(*stages):
    stages = list(stages)
    while stages:
        for stage in list(stages):
            if next(stage, True):
                stages.remove(stage)


def attend_kernel(ends, edge, limit, *refs):
    halos, refs = (refs[:11], refs[11:]) if edge else (refs[:8], refs[8:])
    own0, own1, zlow, zhigh, xlow, xhigh, xzlow, xzhigh, *late = halos
    consts, (out_ref, *refs) = refs[:6], refs[6:]
    x_ref, k_ref, vt_ref, qbd_ref, om_ref, s_ref, p_ref, m_ref, lists, sems, wqT, wvT, *held = refs
    every, gain, shift_ref, w_qkv, wo, bo = held
    copies = list(zip(consts, held)) + [
        (own0, x_ref.at[1, 1:5, 1:5]),
        (own1, x_ref.at[2, 1:5, 1:5]),
        (zlow, x_ref.at[1:3, 1:5, 0]),
        (zhigh, x_ref.at[1:3, 1:5, 5]),
        (xlow, x_ref.at[0, 1:5, 1:5]),
        (xhigh, x_ref.at[3, 1:5, 1:5]),
        (xzlow.at[0], x_ref.at[0, 1:5, 0]),
        (xzlow.at[1], x_ref.at[0, 1:5, 5]),
        (xzhigh.at[0], x_ref.at[3, 1:5, 0]),
        (xzhigh.at[1], x_ref.at[3, 1:5, 5]),
    ]
    if edge:
        done = late.pop()
        copies += list(zip(late, (x_ref.at[:, 0], x_ref.at[:, 5])))
    copies = [pltpu.make_async_copy(a, b, sems.at[i]) for i, (a, b) in enumerate(copies)]
    for copy in copies:
        copy.start()

    spots = [lax.axis_index(axis) for axis in AXES]
    first = [(spot == 0).astype(jnp.int32) for spot in spots]
    last = [(spot == end).astype(jnp.int32) for spot, end in zip(spots, ends)]

    def place(dim, inner, i):
        out = jnp.where(i == 0, first[dim], jnp.where(i == inner + 1, last[dim], 0))
        return 1 - out, jnp.where(out == 0, i, jnp.where(i == 0, 1, inner))

    for copy in copies[:4]:
        copy.wait()
    wqT[...] = w_qkv[:, :256].astype(f32).T.astype(bf)
    wvT[...] = w_qkv[:, 512:].astype(f32).T.astype(bf)
    held_by = every.shape[0]
    entries = 2048.0 * 8.0 * (256 // held_by)
    rows = every[...]
    means = jnp.sum(rows, axis=0, keepdims=True) * (1.0 / held_by)
    apart = rows - means
    spread = jnp.sum(apart * apart, axis=0, keepdims=True)
    first_of = (iota((128, 256), 0) == iota((128, 256), 1) // 8).astype(f32)
    second_of = (iota((128, 256), 0) == iota((128, 256), 1) // 8 + 32).astype(f32)
    means8, spread8 = jnp.broadcast_to(means, (8, 128)), jnp.broadcast_to(spread, (8, 128))
    mean = exact_dot(means8, first_of)[:1]
    var = (exact_dot(means8, second_of)[:1] * (held_by / entries) + exact_dot(spread8, first_of)[:1]) * (1.0 / held_by)
    mul = lax.rsqrt(var + 1e-06) * gain[...]
    shift = shift_ref[...]

    bys = (0, 3) if edge else (1, 2)

    def sort(i, counts):
        deep, flat = counts
        bx, k, bz = i // 8, (i // 4) % 2, i % 4
        by = k * 3 if edge else k + 1
        spot = bx * 16 + by * 4 + bz
        lists[0, deep] = spot
        lists[1, flat] = spot
        is_deep = (limit[bx, by, bz] != 0).astype(jnp.int32)
        return deep + is_deep, flat + 1 - is_deep

    zero = jnp.int32(0)
    deep, flat = lax.fori_loop(0, 16, sort, (zero, zero))

    own_head = iota((256, 512), 0) // 32 == iota((256, 512), 1) // 64
    diag = iota((128, 256), 0) // 32 == iota((128, 256), 1) // 64
    for copy in copies[4:16]:
        copy.wait()

    def normed(cells):
        return ((cells.astype(f32) - mean) * mul + shift).astype(bf)

    lane = iota((1, 256), 1) // 64
    marks = jnp.zeros((1, 256), f32)
    for i in range(4):
        marks = jnp.where(lane == i, place(0, 2, i)[0].astype(f32), marks)
    tick = iota((16, 256), 0) == 0

    def prep_column(c, carry):
        y, z = c // 6, c % 6
        (y_in, y_from), (z_in, z_from) = place(1, 4, y), place(2, 4, z)
        n = normed(
            jnp.concatenate([x_ref[place(0, 2, i)[1], y_from, z_from] for i in range(4)], axis=0)
        )
        k_ref[c] = jnp.dot(n, w_qkv[:, 256:512], preferred_element_type=f32).astype(bf)
        valid = marks * (y_in * z_in).astype(f32)
        vt = lax.dot_general(wvT[...], n, NT, preferred_element_type=f32) * valid
        ones = jnp.where(tick, jnp.broadcast_to(valid, (16, 256)), 0.0)
        for g in range(2):
            t = jnp.concatenate([vt[g * 128 : (g + 1) * 128], ones], axis=0)
            vt_ref[0, c, g] = t[:, :192].astype(bf)
            vt_ref[1, c, g] = pltpu.roll(t, 192, 1)[:, :192].astype(bf)
        return carry

    lax.fori_loop(6, 30, prep_column, 0, unroll=24)

    def prep_query(i, carry):
        bx, k, bz = i // 8, (i // 4) % 2, i % 4
        by = k * 3 if edge else k + 1
        n = normed(x_ref[bx + 1, by + 1, bz + 1])
        q = lax.dot_general(wqT[...], jnp.concatenate([n] * 4, axis=0), NT, preferred_element_type=f32) * SCALE
        qbd_ref[bx * 16 + by * 4 + bz] = jnp.where(own_head, jnp.concatenate([q, q], axis=1), 0.0).astype(bf)
        return carry

    lax.fori_loop(0, 16, prep_query, 0, unroll=16)
    if edge:
        for copy in copies[16:]:
            copy.wait()
        lax.fori_loop(0, 12, lambda t, carry: prep_column(jnp.where(t < 6, t, t + 24), carry), 0, unroll=12)

    def columns(i, cols):
        by, bz = (i // 4) % 4, i % 4
        return [(by + dy) * 6 + bz + dz for dy, dz in cols]

    def scores(i, cols):
        rows = pl.ds(pl.multiple_of(i // 16 * 64, 64), 192)
        q, m, spots = qbd_ref[i], None, columns(i, cols)
        for j in range(0, len(cols), 3):
            keys = jnp.concatenate([k_ref[c, rows] for c in spots[j : j + 3]], axis=0)
            s = jnp.dot(keys, q, preferred_element_type=f32)
            s_ref[j * 192 : (j + 3) * 192] = s
            top = jnp.max(s.reshape(-1, 8, 512), axis=0)
            m = top if m is None else jnp.maximum(m, top)
            yield False
        m_ref[...] = jnp.broadcast_to(jnp.max(m, axis=0, keepdims=True), (8, 512))

    def weights(cols):
        top = m_ref[...][:1]
        for j in range(0, len(cols), 3):
            part = slice(j * 192, (j + 3) * 192)
            p_ref[part] = jnp.exp2(s_ref[part] - top).astype(bf)
            yield False

    def mix(i, cols):
        o = [None, None]
        for j, c in enumerate(columns(i, cols)):
            for g in range(2):
                part = jnp.dot(
                    vt_ref[i // 16, c, g],
                    p_ref[j * 192 : (j + 1) * 192, g * 256 : (g + 1) * 256],
                    preferred_element_type=f32,
                )
                o[g] = part if o[g] is None else o[g] + part
            if j % 3 == 2:
                yield False
        for g in range(2):
            om_ref[i, g] = jnp.where(diag, o[g][:128] * (1.0 / o[g][128:129]), 0.0).astype(bf)

    def run(which, count, cols):
        def spot(t):
            return lists[which, jnp.clip(t, 0, count - 1)]

        def step(t, carry):
            interleave(mix(spot(t - 2), cols), weights(cols), scores(spot(t), cols))
            return carry

        @pl.when(count > 0)
        def _():
            interleave(scores(spot(0), cols))
            interleave(weights(cols), scores(spot(1), cols))
            lax.fori_loop(2, count, step, 0)
            interleave(mix(spot(count - 2), cols), weights(cols))
            interleave(mix(spot(count - 1), cols))

    run(0, deep, [(dy, dz) for dz in range(3) for dy in range(3)])
    run(1, flat, [(dy, 1) for dy in range(3)])

    pick = jnp.where(iota((64, 256), 0) == iota((64, 256), 1) % 64, 1.0, 0.0).astype(bf)
    if edge:
        out_ref[:, 4:12] = done[...]

    def finish(i, carry):
        bx, k = i // 2, i % 2
        by = k * 3 if edge else k + 1
        spot = bx * 16 + by * 4
        mixed = [
            jnp.concatenate(
                [lax.dot_general(pick, om_ref[spot + bz, g], NT, preferred_element_type=f32).astype(bf) for g in range(2)],
                axis=1,
            )
            for bz in range(4)
        ]
        out = jnp.dot(jnp.concatenate(mixed, axis=0), wo[...], preferred_element_type=f32) + bo[...]
        y0 = by * 4 if edge else k * 4
        for x in range(4):
            for pair in range(2):
                parts = [out[b * 64 + x * 16 + pair * 8 : b * 64 + x * 16 + pair * 8 + 8] for b in range(4)]
                for which, join in enumerate((low_rows, high_rows)):
                    line = jnp.concatenate([join(parts[0], parts[1]), join(parts[2], parts[3])], axis=0)
                    out_ref[bx * 4 + x, y0 + pair * 2 + which] = line.astype(bf)
        return carry

    lax.fori_loop(0, 4, finish, 0, unroll=4)


def attend(ends, edge, limit, halos, *consts):
    out_y = 16 if edge else 8
    return pl.pallas_call(
        functools.partial(attend_kernel, ends, edge),
        out_shape=jax.ShapeDtypeStruct((8, out_y, 16, 256), bf),
        in_specs=[SMEM] + [VMEM if half.shape[0] == 8 else HBM for half in halos] + [HBM] * len(consts),
        out_specs=VMEM,
        scratch_shapes=[
            pltpu.VMEM((4, 6, 6, 64, 256), bf),
            pltpu.VMEM((36, 256, 256), bf),
            pltpu.VMEM((2, 36, 2, 144, 192), bf),
            pltpu.VMEM((32, 256, 512), bf),
            pltpu.VMEM((32, 2, 128, 256), bf),
            pltpu.VMEM((1728, 512), f32),
            pltpu.VMEM((1728, 512), bf),
            pltpu.VMEM((8, 512), f32),
            pltpu.SMEM((2, 17), jnp.int32),
            pltpu.SemaphoreType.DMA((18,)),
            pltpu.VMEM((256, 256), bf),
            pltpu.VMEM((256, 256), bf),
        ]
        + [pltpu.VMEM(const.shape, const.dtype) for const in consts],
        compiler_params=pltpu.CompilerParams(vmem_limit_bytes=50 * 2**20),
        cost_estimate=pl.CostEstimate(flops=15 * 10**9, bytes_accessed=8 * 10**6, transcendentals=14 * 10**6),
    )(limit, *halos, *consts)


def swap(low, high, axis):
    count = lax.axis_size(axis)
    up = [(i, i + 1) for i in range(count - 1)]
    down = [(i + 1, i) for i in range(count - 1)]
    return lax.ppermute(high, axis, up), lax.ppermute(low, axis, down)


def on_device(latent, norm_gain, norm_shift, w_qkv, w_out, b_out, depth_limit):
    zlow, zhigh = swap(*z_faces(latent), "gz")
    own0, own1, held = arrange(latent)
    xlow, xhigh = swap(own0, own1, "gx")
    step = 1
    while step < lax.axis_size("gy"):
        pairs = [(i, i ^ step) for i in range(lax.axis_size("gy"))]
        held = jnp.concatenate([held, lax.ppermute(held, "gy", pairs)], axis=0)
        step *= 2
    rest = ("gx", "gz")
    rows = jax.ShapeDtypeStruct((lax.axis_size(rest), 128), f32)
    kernel = functools.partial(edges_kernel, float(latent.size // 32))
    *edges, rows = faces(kernel, (2, 4, 64, 256), (held, zlow, zhigh), rows)
    xzlow, xzhigh = swap(*edges, "gx")
    every = lax.all_to_all(rows, rest, 0, 0, tiled=True)
    near = (own0, own1, zlow, zhigh, xlow, xhigh, xzlow, xzhigh)
    ylow, yhigh = swap(*faces(y_faces_kernel, (4, 6, 64, 256), near), "gy")
    consts = (
        every,
        norm_gain[None],
        norm_shift[None],
        w_qkv,
        w_out,
        b_out[None],
    )
    ends = tuple(lax.axis_size(axis) - 1 for axis in AXES)
    middle = attend(ends, False, depth_limit, near, *consts)
    return attend(ends, True, depth_limit, near + (ylow, yhigh, middle), *consts)


def solution(mesh):
    placed = (P("gx", "gy", "gz", None), P(), P(), P(), P(), P(), P("gx", "gy", "gz"))
    return jax.shard_map(
        on_device, mesh=mesh, in_specs=placed, out_specs=P("gx", "gy", "gz", None), check_vma=False
    )
```

profile of v0, /device:TPU:16, one launch (start us, length us, event | category | flops | bytes accessed | tf_op | source)
XLA Modules:
  0.0 96.6 jit_solution(10578933199728887935)
XLA Ops:
  0.0 1.2 %copy-done = bf16[8,16,16,256]{3,2,1,0:T(8,128)(2,1)S(1)} copy-done((bf16[8,16,16,256]{3,2,1,0:T(8,128)(2,1)S(1)}, bf16[8,16,16,256]{3,2,1,0:T(8,128)(2,1)}, u32[]{:S(2)}) %copy-start) | copy-done | bytes 1048600
  1.2 0.2 shard_map.74
  1.4 3.8 %collective-permute-start = (bf16[2,4,64,256]{3,2,1,0:T(8,128)(2,1)S(1)}, bf16[2,4,64,256]{3,2,1,0:T(8,128)(2,1)S(1)}, u32[]{:S(2)}, u32[]{:S(2)}) collective-permute-start(bf16[2,4,64,256]{3,2,1,0:T(8,128)(2,1)S(1)} %get-tuple-element.17), channel_id=1, source_target_pairs={{0,1},{1,2},{2,3},{3,4},{4,5},{5,6},{6,7},{8,9},{9,10},{10,11},{11... | collective-permute-start | bytes 786440 | tf_op jit(solution)/shard_map/ppermute | solution.py:377
  5.2 1.3 %collective-permute-start.1 = (bf16[2,4,64,256]{3,2,1,0:T(8,128)(2,1)S(1)}, bf16[2,4,64,256]{3,2,1,0:T(8,128)(2,1)S(1)}, u32[]{:S(2)}, u32[]{:S(2)}) collective-permute-start(bf16[2,4,64,256]{3,2,1,0:T(8,128)(2,1)S(1)} %get-tuple-element.18), channel_id=1, source_target_pairs={{1,0},{2,1},{3,2},{4,3},{5,4},{6,5},{7,6},{9,8},{10,9},{11,10},{12... | collective-permute-start | bytes 786440 | tf_op jit(solution)/shard_map/ppermute | solution.py:377
  6.5 1.5 %shard_map.73 = (bf16[4,4,64,256]{3,2,1,0:T(8,128)(2,1)S(1)}, bf16[4,4,64,256]{3,2,1,0:T(8,128)(2,1)S(1)}, f32[8,128]{1,0:T(8,128)S(1)}) custom-call(bf16[8,16,16,256]{3,2,1,0:T(8,128)(2,1)S(1)} %copy-done), custom_call_target="tpu_custom_call" | custom-call | tf_op jit(solution)/shard_map/pallas_call | solution.py:98
  8.0 1.3 %collective-permute-start.3 = (bf16[4,4,64,256]{3,2,1,0:T(8,128)(2,1)S(1)}, bf16[4,4,64,256]{3,2,1,0:T(8,128)(2,1)S(1)}, u32[]{:S(2)}, u32[]{:S(2)}) collective-permute-start(bf16[4,4,64,256]{3,2,1,0:T(8,128)(2,1)S(1)} %get-tuple-element.15.own0.refs_0_), channel_id=1, source_target_pairs={{32,0},{64,32},{96,64},{128,96},{160,128},{192,160},{224,192},{33,... | collective-permute-start | bytes 1572872 | tf_op jit(solution)/shard_map/ppermute | solution.py:377
  9.3 3.1 %collective-permute-start.2 = (bf16[4,4,64,256]{3,2,1,0:T(8,128)(2,1)S(1)}, bf16[4,4,64,256]{3,2,1,0:T(8,128)(2,1)S(1)}, u32[]{:S(2)}, u32[]{:S(2)}) collective-permute-start(bf16[4,4,64,256]{3,2,1,0:T(8,128)(2,1)S(1)} %get-tuple-element.16.own1.refs_1_), channel_id=1, source_target_pairs={{0,32},{32,64},{64,96},{96,128},{128,160},{160,192},{192,224},{1,3... | collective-permute-start | bytes 1572872 | tf_op jit(solution)/shard_map/ppermute | solution.py:377
  12.4 1.4 %collective-permute-start.4 = (f32[8,128]{1,0:T(8,128)S(1)}, f32[8,128]{1,0:T(8,128)S(1)}, u32[]{:S(2)}, u32[]{:S(2)}) collective-permute-start(f32[8,128]{1,0:T(8,128)S(1)} %get-tuple-element.19), channel_id=1, source_target_pairs={{0,8},{8,0},{16,24},{24,16},{1,9},{9,1},{17,25},{25,17},{2,10},{10... | collective-permute-start | bytes 12296 | tf_op jit(solution)/shard_map/ppermute | solution.py:387
  13.8 2.3 %collective-permute-done.4 = f32[8,128]{1,0:T(8,128)S(1)} collective-permute-done((f32[8,128]{1,0:T(8,128)S(1)}, f32[8,128]{1,0:T(8,128)S(1)}, u32[]{:S(2)}, u32[]{:S(2)}) %collective-permute-start.4) | collective-permute-done | bytes 4128 | tf_op jit(solution)/shard_map/ppermute | solution.py:387
  16.1 0.3 collective-permute-start.5
  16.4 4.8 %collective-permute-done.5 = f32[16,128]{1,0:T(8,128)S(1)} collective-permute-done((f32[16,128]{1,0:T(8,128)S(1)}, f32[16,128]{1,0:T(8,128)S(1)}, u32[]{:S(2)}, u32[]{:S(2)}) %collective-permute-start.5) | collective-permute-done | bytes 8224 | tf_op jit(solution)/shard_map/ppermute | solution.py:387
  21.3 2.2 %collective-permute-done.1.zhigh.refs_3_ = bf16[2,4,64,256]{3,2,1,0:T(8,128)(2,1)S(1)} collective-permute-done((bf16[2,4,64,256]{3,2,1,0:T(8,128)(2,1)S(1)}, bf16[2,4,64,256]{3,2,1,0:T(8,128)(2,1)S(1)}, u32[]{:S(2)}, u32[]{:S(2)}) %collective-permute-start.1) | collective-permute-done | bytes 262176 | tf_op jit(solution)/shard_map/ppermute | solution.py:377
  23.5 0.7 shard_map.75
  24.2 1.3 %collective-permute-start.6 = (bf16[2,4,64,256]{3,2,1,0:T(8,128)(2,1)}, bf16[2,4,64,256]{3,2,1,0:T(8,128)(2,1)S(1)}, u32[]{:S(2)}, u32[]{:S(2)}) collective-permute-start(bf16[2,4,64,256]{3,2,1,0:T(8,128)(2,1)} %get-tuple-element.20), channel_id=1, source_target_pairs={{0,32},{32,64},{64,96},{96,128},{128,160},{160,192},{192,224},{1,3... | collective-permute-start | bytes 786440 | tf_op jit(solution)/shard_map/ppermute | solution.py:377
  25.5 1.3 %collective-permute-start.7 = (bf16[2,4,64,256]{3,2,1,0:T(8,128)(2,1)S(1)}, bf16[2,4,64,256]{3,2,1,0:T(8,128)(2,1)S(1)}, u32[]{:S(2)}, u32[]{:S(2)}) collective-permute-start(bf16[2,4,64,256]{3,2,1,0:T(8,128)(2,1)S(1)} %get-tuple-element.21), channel_id=1, source_target_pairs={{32,0},{64,32},{96,64},{128,96},{160,128},{192,160},{224,192},{33,... | collective-permute-start | bytes 786440 | tf_op jit(solution)/shard_map/ppermute | solution.py:377
  26.8 16.4 %all-to-all-start = ((f32[64,1,128]{2,1,0:T(1,128)}), f32[64,1,128]{2,1,0:T(1,128)S(1)}, u32[]{:S(2)}, u32[]{:S(2)}) async-start(f32[64,1,128]{2,1,0:T(1,128)} %bitcast.1), calls=%async_computation | async-start | bytes 65536 | tf_op jit(solution)/shard_map/all_to_all | solution.py:394
  43.2 0.0 collective-permute-done.3.xhigh.refs_5_
  43.3 0.0 collective-permute-done.6.xzlow.refs_6_
  43.3 0.0 collective-permute-done.7.xzhigh.refs_7_
  43.3 0.0 copy-start.4
  43.3 0.0 copy-start.7
  43.3 0.0 copy-start.8
  43.3 1.2 %shard_map.76 = (bf16[4,6,64,256]{3,2,1,0:T(8,128)(2,1)}, bf16[4,6,64,256]{3,2,1,0:T(8,128)(2,1)}) custom-call(bf16[4,4,64,256]{3,2,1,0:T(8,128)(2,1)S(1)} %get-tuple-element.15.own0.refs_0_, bf16[4,4,64,256]{3,2,1,0:T(8,128)(2,1)S(1)} %get-tuple-element.16.own1.refs_1_, bf16[2,4,64,256]{3,2,1,0:T(8,128)(2,1)S(1)} %collective-permute-done.zlow.refs_2_, ...), custom_call_target="tpu_custom_call" | custom-call | tf_op jit(solution)/shard_map/pallas_call | solution.py:132
  44.6 3.2 %collective-permute-start.8 = (bf16[4,6,64,256]{3,2,1,0:T(8,128)(2,1)}, bf16[4,6,64,256]{3,2,1,0:T(8,128)(2,1)}, u32[]{:S(2)}, u32[]{:S(2)}) collective-permute-start(bf16[4,6,64,256]{3,2,1,0:T(8,128)(2,1)} %get-tuple-element.22), channel_id=1, source_target_pairs={{0,8},{8,16},{16,24},{1,9},{9,17},{17,25},{2,10},{10,18},{18,26},{... | collective-permute-start | bytes 2359304 | tf_op jit(solution)/shard_map/ppermute | solution.py:377
  47.8 0.0 copy-start.5
  47.8 2.7 %collective-permute-start.9 = (bf16[4,6,64,256]{3,2,1,0:T(8,128)(2,1)}, bf16[4,6,64,256]{3,2,1,0:T(8,128)(2,1)}, u32[]{:S(2)}, u32[]{:S(2)}) collective-permute-start(bf16[4,6,64,256]{3,2,1,0:T(8,128)(2,1)} %get-tuple-element.23), channel_id=1, source_target_pairs={{8,0},{16,8},{24,16},{9,1},{17,9},{25,17},{10,2},{18,10},{26,18},{... | collective-permute-start | bytes 2359304 | tf_op jit(solution)/shard_map/ppermute | solution.py:377
  50.4 2.4 %all-to-all-done = f32[64,1,128]{2,1,0:T(1,128)S(1)} async-done(((f32[64,1,128]{2,1,0:T(1,128)}), f32[64,1,128]{2,1,0:T(1,128)S(1)}, u32[]{:S(2)}, u32[]{:S(2)}) %all-to-all-start) | async-done | bytes 32800 | tf_op jit(solution)/shard_map/all_to_all | solution.py:394
  52.9 0.7 copy-done.6
  53.5 1.0 %copy-done.3 = bf16[256,768]{1,0:T(8,128)(2,1)S(1)} copy-done((bf16[256,768]{1,0:T(8,128)(2,1)S(1)}, bf16[256,768]{1,0:T(8,128)(2,1)}, u32[]{:S(2)}) %copy-start.3) | copy-done | bytes 393240
  54.5 19.6 %shard_map.77.refs_10_ = bf16[8,8,16,256]{3,2,1,0:T(8,128)(2,1)S(1)} custom-call(s32[2,4,4]{2,1,0:T(4,128)S(1)} %copy-done.5, bf16[4,4,64,256]{3,2,1,0:T(8,128)(2,1)S(1)} %get-tuple-element.15.own0.refs_0_, bf16[4,4,64,256]{3,2,1,0:T(8,128)(2,1)S(1)} %get-tuple-element.16.own1.refs_1_, bf16[2,4,64,256]{3,2,1,0:T(8,128)(2,1)S(1)} %collective-permute-done.zlow.refs_2_, ...), custom_call_target="tpu_custom_call" | custom-call | flops 15000000512 | bytes 8000000 | tf_op jit(solution)/shard_map/pallas_call | solution.py:348
  74.2 0.8 copy-done.9
  75.0 21.4 %shard_map.78 = bf16[8,16,16,256]{3,2,1,0:T(8,128)(2,1)} custom-call(s32[2,4,4]{2,1,0:T(4,128)S(1)} %copy-done.5, bf16[4,4,64,256]{3,2,1,0:T(8,128)(2,1)S(1)} %get-tuple-element.15.own0.refs_0_, bf16[4,4,64,256]{3,2,1,0:T(8,128)(2,1)S(1)} %get-tuple-element.16.own1.refs_1_, bf16[2,4,64,256]{3,2,1,0:T(8,128)(2,1)S(1)} %collective-permute-done.zlow.refs_2_, ...), custom_call_target="tpu_custom_call" | custom-call | flops 15000000512 | bytes 8000000 | tf_op jit(solution)/shard_map/pallas_call | solution.py:348
  (18 shorter events, 0.0 us)
Async XLA Ops:
  0.0 1.2 %copy-start = (bf16[8,16,16,256]{3,2,1,0:T(8,128)(2,1)S(1)}, bf16[8,16,16,256]{3,2,1,0:T(8,128)(2,1)}, u32[]{:S(2)}) copy-start(bf16[8,16,16,256]{3,2,1,0:T(8,128)(2,1)} %x_ref.3) | copy-start | bytes 3145732
  1.4 19.9 %collective-permute-start = (bf16[2,4,64,256]{3,2,1,0:T(8,128)(2,1)S(1)}, bf16[2,4,64,256]{3,2,1,0:T(8,128)(2,1)S(1)}, u32[]{:S(2)}, u32[]{:S(2)}) collective-permute-start(bf16[2,4,64,256]{3,2,1,0:T(8,128)(2,1)S(1)} %get-tuple-element.17), channel_id=1, source_target_pairs={{0,1},{1,2},{2,3},{3,4},{4,5},{5,6},{6,7},{8,9},{9,10},{10,11},{11... | collective-permute-start | bytes 786440 | tf_op jit(solution)/shard_map/ppermute | solution.py:377
  5.2 18.3 %collective-permute-start.1 = (bf16[2,4,64,256]{3,2,1,0:T(8,128)(2,1)S(1)}, bf16[2,4,64,256]{3,2,1,0:T(8,128)(2,1)S(1)}, u32[]{:S(2)}, u32[]{:S(2)}) collective-permute-start(bf16[2,4,64,256]{3,2,1,0:T(8,128)(2,1)S(1)} %get-tuple-element.18), channel_id=1, source_target_pairs={{1,0},{2,1},{3,2},{4,3},{5,4},{6,5},{7,6},{9,8},{10,9},{11,10},{12... | collective-permute-start | bytes 786440 | tf_op jit(solution)/shard_map/ppermute | solution.py:377
  8.0 35.2 %collective-permute-start.3 = (bf16[4,4,64,256]{3,2,1,0:T(8,128)(2,1)S(1)}, bf16[4,4,64,256]{3,2,1,0:T(8,128)(2,1)S(1)}, u32[]{:S(2)}, u32[]{:S(2)}) collective-permute-start(bf16[4,4,64,256]{3,2,1,0:T(8,128)(2,1)S(1)} %get-tuple-element.15.own0.refs_0_), channel_id=1, source_target_pairs={{32,0},{64,32},{96,64},{128,96},{160,128},{192,160},{224,192},{33,... | collective-permute-start | bytes 1572872 | tf_op jit(solution)/shard_map/ppermute | solution.py:377
  9.3 33.9 %collective-permute-start.2 = (bf16[4,4,64,256]{3,2,1,0:T(8,128)(2,1)S(1)}, bf16[4,4,64,256]{3,2,1,0:T(8,128)(2,1)S(1)}, u32[]{:S(2)}, u32[]{:S(2)}) collective-permute-start(bf16[4,4,64,256]{3,2,1,0:T(8,128)(2,1)S(1)} %get-tuple-element.16.own1.refs_1_), channel_id=1, source_target_pairs={{0,32},{32,64},{64,96},{96,128},{128,160},{160,192},{192,224},{1,3... | collective-permute-start | bytes 1572872 | tf_op jit(solution)/shard_map/ppermute | solution.py:377
  12.4 3.7 %collective-permute-start.4 = (f32[8,128]{1,0:T(8,128)S(1)}, f32[8,128]{1,0:T(8,128)S(1)}, u32[]{:S(2)}, u32[]{:S(2)}) collective-permute-start(f32[8,128]{1,0:T(8,128)S(1)} %get-tuple-element.19), channel_id=1, source_target_pairs={{0,8},{8,0},{16,24},{24,16},{1,9},{9,1},{17,25},{25,17},{2,10},{10... | collective-permute-start | bytes 12296 | tf_op jit(solution)/shard_map/ppermute | solution.py:387
  16.1 5.2 %collective-permute-start.5 = (f32[16,128]{1,0:T(8,128)S(1)}, f32[16,128]{1,0:T(8,128)S(1)}, u32[]{:S(2)}, u32[]{:S(2)}) collective-permute-start(f32[16,128]{1,0:T(8,128)S(1)} %pad_maximum_fusion.1), channel_id=1, source_target_pairs={{0,16},{8,24},{16,0},{24,8},{1,17},{9,25},{17,1},{25,9},{2,18},{10... | collective-permute-start | bytes 24584 | tf_op jit(solution)/shard_map/ppermute | solution.py:387
  24.2 19.0 %collective-permute-start.6 = (bf16[2,4,64,256]{3,2,1,0:T(8,128)(2,1)}, bf16[2,4,64,256]{3,2,1,0:T(8,128)(2,1)S(1)}, u32[]{:S(2)}, u32[]{:S(2)}) collective-permute-start(bf16[2,4,64,256]{3,2,1,0:T(8,128)(2,1)} %get-tuple-element.20), channel_id=1, source_target_pairs={{0,32},{32,64},{64,96},{96,128},{128,160},{160,192},{192,224},{1,3... | collective-permute-start | bytes 786440 | tf_op jit(solution)/shard_map/ppermute | solution.py:377
  25.5 17.7 %collective-permute-start.7 = (bf16[2,4,64,256]{3,2,1,0:T(8,128)(2,1)S(1)}, bf16[2,4,64,256]{3,2,1,0:T(8,128)(2,1)S(1)}, u32[]{:S(2)}, u32[]{:S(2)}) collective-permute-start(bf16[2,4,64,256]{3,2,1,0:T(8,128)(2,1)S(1)} %get-tuple-element.21), channel_id=1, source_target_pairs={{32,0},{64,32},{96,64},{128,96},{160,128},{192,160},{224,192},{33,... | collective-permute-start | bytes 786440 | tf_op jit(solution)/shard_map/ppermute | solution.py:377
  26.8 26.0 %all-to-all-start = ((f32[64,1,128]{2,1,0:T(1,128)}), f32[64,1,128]{2,1,0:T(1,128)S(1)}, u32[]{:S(2)}, u32[]{:S(2)}) async-start(f32[64,1,128]{2,1,0:T(1,128)} %bitcast.1), calls=%async_computation | async-start | bytes 65536 | tf_op jit(solution)/shard_map/all_to_all | solution.py:394
  43.2 1.3 %copy-start.1 = (bf16[4,4,64,256]{3,2,1,0:T(8,128)(2,1)}, bf16[4,4,64,256]{3,2,1,0:T(8,128)(2,1)S(1)}, u32[]{:S(2)}) copy-start(bf16[4,4,64,256]{3,2,1,0:T(8,128)(2,1)S(1)} %collective-permute-done.3.xhigh.refs_5_) | copy-start | bytes 1572868
  43.3 9.6 %copy-start.4 = (bf16[256,256]{1,0:T(8,128)(2,1)S(1)}, bf16[256,256]{1,0:T(8,128)(2,1)}, u32[]{:S(2)}) copy-start(bf16[256,256]{1,0:T(8,128)(2,1)} %refs_15_.1) | copy-start | bytes 393220
  43.3 9.5 %copy-start.7 = (f32[256]{0:T(256)S(1)}, f32[256]{0:T(256)}, u32[]{:S(2)}) copy-start(f32[256]{0:T(256)} %param.9) | copy-start | bytes 3076
  43.3 9.5 %copy-start.8 = (f32[256]{0:T(256)S(1)}, f32[256]{0:T(256)}, u32[]{:S(2)}) copy-start(f32[256]{0:T(256)} %param.12) | copy-start | bytes 3076
  44.6 30.4 %collective-permute-start.8 = (bf16[4,6,64,256]{3,2,1,0:T(8,128)(2,1)}, bf16[4,6,64,256]{3,2,1,0:T(8,128)(2,1)}, u32[]{:S(2)}, u32[]{:S(2)}) collective-permute-start(bf16[4,6,64,256]{3,2,1,0:T(8,128)(2,1)} %get-tuple-element.22), channel_id=1, source_target_pairs={{0,8},{8,16},{16,24},{1,9},{9,17},{17,25},{2,10},{10,18},{18,26},{... | collective-permute-start | bytes 2359304 | tf_op jit(solution)/shard_map/ppermute | solution.py:377
  47.8 5.1 %copy-start.5 = (s32[2,4,4]{2,1,0:T(4,128)S(1)}, s32[2,4,4]{2,1,0:T(4,128)}, u32[]{:S(2)}) copy-start(s32[2,4,4]{2,1,0:T(4,128)} %limit.3) | copy-start | bytes 388
  47.8 27.2 %collective-permute-start.9 = (bf16[4,6,64,256]{3,2,1,0:T(8,128)(2,1)}, bf16[4,6,64,256]{3,2,1,0:T(8,128)(2,1)}, u32[]{:S(2)}, u32[]{:S(2)}) collective-permute-start(bf16[4,6,64,256]{3,2,1,0:T(8,128)(2,1)} %get-tuple-element.23), channel_id=1, source_target_pairs={{8,0},{16,8},{24,16},{9,1},{17,9},{25,17},{10,2},{18,10},{26,18},{... | collective-permute-start | bytes 2359304 | tf_op jit(solution)/shard_map/ppermute | solution.py:377
  52.8 0.7 copy-start.6
  53.5 1.0 %copy-start.3 = (bf16[256,768]{1,0:T(8,128)(2,1)S(1)}, bf16[256,768]{1,0:T(8,128)(2,1)}, u32[]{:S(2)}) copy-start(bf16[256,768]{1,0:T(8,128)(2,1)} %refs_14_.1) | copy-start | bytes 1179652
  54.5 20.5 %copy-start.2 = (bf16[4,4,64,256]{3,2,1,0:T(8,128)(2,1)S(1)}, bf16[4,4,64,256]{3,2,1,0:T(8,128)(2,1)}, u32[]{:S(2)}) copy-start(bf16[4,4,64,256]{3,2,1,0:T(8,128)(2,1)} %copy-done.1) | copy-start | bytes 1572868
  74.2 0.8 copy-start.9
where the time goes:
time: 96.8 us; the launch traced here: 96.6 us
  Pallas kernels  44.7 us (46%)
  starting transfers between devices  36 us (37%)
  waiting for transfers between devices  11.8 us (12%)
  local copies, waits for them, and re-layouts  3.7 us (4%)
    pallas_call x2, Pallas kernels, attend(): pl.pallas_call(functools.partial(attend_kernel, ends, edge), out_shape=ja...  41.1 us
    ppermute x8, starting transfers between devices, swap(): return (lax.ppermute(high, axis, up), lax.ppermute(low, axis, down))  17.9 us
    all_to_all x1, starting transfers between devices, on_device(): every = lax.all_to_all(rows, rest, 0, 0, tiled=True)  16.4 us
    ppermute x2, waiting for transfers between devices, on_device(): held = jnp.concatenate([held, lax.ppermute(held, 'gy', pairs)], axis=0)  7.14 us
    unnamed x20, local copies, waits for them, and re-layouts  3.7 us
    all_to_all x1, waiting for transfers between devices, on_device(): every = lax.all_to_all(rows, rest, 0, 0, tiled=True)  2.4 us
    ppermute x8, waiting for transfers between devices, swap(): return (lax.ppermute(high, axis, up), lax.ppermute(low, axis, down))  2.24 us
    pallas_call x2, Pallas kernels, faces(): pl.pallas_call(kernel, out_shape=[face, face, *more], in_specs=[VMEM] * l...  1.99 us
  transfers between devices with their start and end apart: 11, of which 4 were waited for; matrix products, arithmetic and copies ran while one was open for 0% of the time, Pallas kernels for 24%

commit v1 on v0

--- a/solution.py
+++ b/solution.py
@@ -262,58 +262,63 @@
         by, bz = (i // 4) % 4, i % 4
         return [(by + dy) * 6 + bz + dz for dy, dz in cols]
 
-    def scores(i, cols):
-        rows = pl.ds(pl.multiple_of(i // 16 * 64, 64), 192)
-        q, m, spots = qbd_ref[i], None, columns(i, cols)
-        for j in range(0, len(cols), 3):
-            keys = jnp.concatenate([k_ref[c, rows] for c in spots[j : j + 3]], axis=0)
-            s = jnp.dot(keys, q, preferred_element_type=f32)
-            s_ref[j * 192 : (j + 3) * 192] = s
-            top = jnp.max(s.reshape(-1, 8, 512), axis=0)
-            m = top if m is None else jnp.maximum(m, top)
-            yield False
-        m_ref[...] = jnp.broadcast_to(jnp.max(m, axis=0, keepdims=True), (8, 512))
-
-    def weights(cols):
-        top = m_ref[...][:1]
-        for j in range(0, len(cols), 3):
-            part = slice(j * 192, (j + 3) * 192)
-            p_ref[part] = jnp.exp2(s_ref[part] - top).astype(bf)
-            yield False
-
-    def mix(i, cols):
-        o = [None, None]
-        for j, c in enumerate(columns(i, cols)):
+    def scores(blocks, cols):
+        for k, i in enumerate(blocks):
+            rows = pl.ds(pl.multiple_of(i // 16 * 64, 64), 192)
+            q, m, spots = qbd_ref[i], None, columns(i, cols)
+            for j in range(0, len(cols), 3):
+                keys = jnp.concatenate([k_ref[c, rows] for c in spots[j : j + 3]], axis=0)
+                s = jnp.dot(keys, q, preferred_element_type=f32)
+                s_ref[k * 576 + j * 192 : k * 576 + (j + 3) * 192] = s
+                top = jnp.max(s.reshape(-1, 8, 512), axis=0)
+                m = top if m is None else jnp.maximum(m, top)
+                yield False
+            m_ref[k] = jnp.broadcast_to(jnp.max(m, axis=0, keepdims=True), (8, 512))
+
+    def weights(blocks, cols):
+        for k in range(len(blocks)):
+            top = m_ref[k][:1]
+            for j in range(0, len(cols), 3):
+                part = slice(k * 576 + j * 192, k * 576 + (j + 3) * 192)
+                p_ref[part] = jnp.exp2(s_ref[part] - top).astype(bf)
+                yield False
+
+    def mix(blocks, cols):
+        for k, i in enumerate(blocks):
+            o = [None, None]
+            for j, c in enumerate(columns(i, cols)):
+                for g in range(2):
+                    part = jnp.dot(
+                        vt_ref[i // 16, c, g],
+                        p_ref[k * 576 + j * 192 : k * 576 + (j + 1) * 192, g * 256 : (g + 1) * 256],
+                        preferred_element_type=f32,
+                    )
+                    o[g] = part if o[g] is None else o[g] + part
+                if j % 3 == 2:
+                    yield False
             for g in range(2):
-                part = jnp.dot(
-                    vt_ref[i // 16, c, g],
-                    p_ref[j * 192 : (j + 1) * 192, g * 256 : (g + 1) * 256],
-                    preferred_element_type=f32,
-                )
-                o[g] = part if o[g] is None else o[g] + part
-            if j % 3 == 2:
-                yield False
-        for g in range(2):
-            om_ref[i, g] = jnp.where(diag, o[g][:128] * (1.0 / o[g][128:129]), 0.0).astype(bf)
-
-    def run(which, count, cols):
-        def spot(t):
-            return lists[which, jnp.clip(t, 0, count - 1)]
+                om_ref[i, g] = jnp.where(diag, o[g][:128] * (1.0 / o[g][128:129]), 0.0).astype(bf)
+
+    def run(which, count, cols, width):
+        steps = (count + width - 1) // width
+
+        def spots(t):
+            return [lists[which, jnp.clip(t * width + k, 0, count - 1)] for k in range(width)]
 
         def step(t, carry):
-            interleave(mix(spot(t - 2), cols), weights(cols), scores(spot(t), cols))
+            interleave(mix(spots(t - 2), cols), weights(spots(t - 1), cols), scores(spots(t), cols))
             return carry
 
         @pl.when(count > 0)
         def _():
-            interleave(scores(spot(0), cols))
-            interleave(weights(cols), scores(spot(1), cols))
-            lax.fori_loop(2, count, step, 0)
-            interleave(mix(spot(count - 2), cols), weights(cols))
-            interleave(mix(spot(count - 1), cols))
-
-    run(0, deep, [(dy, dz) for dz in range(3) for dy in range(3)])
-    run(1, flat, [(dy, 1) for dy in range(3)])
+            interleave(scores(spots(0), cols))
+            interleave(weights(spots(0), cols), scores(spots(jnp.minimum(1, steps - 1)), cols))
+            lax.fori_loop(2, steps, step, 0)
+            interleave(mix(spots(jnp.maximum(steps - 2, 0)), cols), weights(spots(steps - 1), cols))
+            interleave(mix(spots(steps - 1), cols))
+
+    run(0, deep, [(dy, dz) for dz in range(3) for dy in range(3)], 1)
+    run(1, flat, [(dy, 1) for dy in range(3)], 2)
 
     pick = jnp.where(iota((64, 256), 0) == iota((64, 256), 1) % 64, 1.0, 0.0).astype(bf)
     if edge:
@@ -358,7 +363,7 @@
             pltpu.VMEM((32, 2, 128, 256), bf),
             pltpu.VMEM((1728, 512), f32),
             pltpu.VMEM((1728, 512), bf),
-            pltpu.VMEM((8, 512), f32),
+            pltpu.VMEM((3, 8, 512), f32),
             pltpu.SMEM((2, 17), jnp.int32),
             pltpu.SemaphoreType.DMA((18,)),
             pltpu.VMEM((256, 256), bf),

time: 96.8 us -> 96.1 us (level)
  the two profiles are of different devices: /device:TPU:16 before, /device:TPU:25 now
where the time goes in v1:
time: 96.1 us; the launch traced here: 95.9 us
  Pallas kernels  44.3 us (46%)
  starting transfers between devices  40.3 us (42%)
  waiting for transfers between devices  7.32 us (8%)
  local copies, waits for them, and re-layouts  3.7 us (4%)
    pallas_call x2, Pallas kernels, attend(): pl.pallas_call(functools.partial(attend_kernel, ends, edge), out_shape=ja...  40.6 us
    ppermute x8, starting transfers between devices, swap(): return (lax.ppermute(high, axis, up), lax.ppermute(low, axis, down))  27 us
    all_to_all x1, starting transfers between devices, on_device(): every = lax.all_to_all(rows, rest, 0, 0, tiled=True)  11.8 us
    ppermute x2, waiting for transfers between devices, on_device(): held = jnp.concatenate([held, lax.ppermute(held, 'gy', pairs)], axis=0)  5.34 us
    unnamed x20, local copies, waits for them, and re-layouts  3.7 us
    pallas_call x2, Pallas kernels, faces(): pl.pallas_call(kernel, out_shape=[face, face, *more], in_specs=[VMEM] * l...  1.99 us
  transfers between devices with their start and end apart: 11, of which 4 were waited for; matrix products, arithmetic and copies ran while one was open for 0% of the time, Pallas kernels for 23%

profile of v1, /device:TPU:25, one launch (start us, length us, event | category | flops | bytes accessed | tf_op | source)
XLA Modules:
  0.0 95.9 jit_solution(6692543199113661787)
XLA Ops:
  0.0 1.2 %copy-done = bf16[8,16,16,256]{3,2,1,0:T(8,128)(2,1)S(1)} copy-done((bf16[8,16,16,256]{3,2,1,0:T(8,128)(2,1)S(1)}, bf16[8,16,16,256]{3,2,1,0:T(8,128)(2,1)}, u32[]{:S(2)}) %copy-start) | copy-done | bytes 1048600
  1.2 0.2 shard_map.74
  1.4 3.6 %collective-permute-start = (bf16[2,4,64,256]{3,2,1,0:T(8,128)(2,1)S(1)}, bf16[2,4,64,256]{3,2,1,0:T(8,128)(2,1)S(1)}, u32[]{:S(2)}, u32[]{:S(2)}) collective-permute-start(bf16[2,4,64,256]{3,2,1,0:T(8,128)(2,1)S(1)} %get-tuple-element.17), channel_id=1, source_target_pairs={{0,1},{1,2},{2,3},{3,4},{4,5},{5,6},{6,7},{8,9},{9,10},{10,11},{11... | collective-permute-start | bytes 786440 | tf_op jit(solution)/shard_map/ppermute | solution.py:382
  4.9 1.3 %collective-permute-start.1 = (bf16[2,4,64,256]{3,2,1,0:T(8,128)(2,1)S(1)}, bf16[2,4,64,256]{3,2,1,0:T(8,128)(2,1)S(1)}, u32[]{:S(2)}, u32[]{:S(2)}) collective-permute-start(bf16[2,4,64,256]{3,2,1,0:T(8,128)(2,1)S(1)} %get-tuple-element.18), channel_id=1, source_target_pairs={{1,0},{2,1},{3,2},{4,3},{5,4},{6,5},{7,6},{9,8},{10,9},{11,10},{12... | collective-permute-start | bytes 786440 | tf_op jit(solution)/shard_map/ppermute | solution.py:382
  6.2 1.5 %shard_map.73 = (bf16[4,4,64,256]{3,2,1,0:T(8,128)(2,1)S(1)}, bf16[4,4,64,256]{3,2,1,0:T(8,128)(2,1)S(1)}, f32[8,128]{1,0:T(8,128)S(1)}) custom-call(bf16[8,16,16,256]{3,2,1,0:T(8,128)(2,1)S(1)} %copy-done), custom_call_target="tpu_custom_call" | custom-call | tf_op jit(solution)/shard_map/pallas_call | solution.py:98
  7.8 2.9 %collective-permute-start.3 = (bf16[4,4,64,256]{3,2,1,0:T(8,128)(2,1)S(1)}, bf16[4,4,64,256]{3,2,1,0:T(8,128)(2,1)S(1)}, u32[]{:S(2)}, u32[]{:S(2)}) collective-permute-start(bf16[4,4,64,256]{3,2,1,0:T(8,128)(2,1)S(1)} %get-tuple-element.15.own0.refs_0_), channel_id=1, source_target_pairs={{32,0},{64,32},{96,64},{128,96},{160,128},{192,160},{224,192},{33,... | collective-permute-start | bytes 1572872 | tf_op jit(solution)/shard_map/ppermute | solution.py:382
  10.6 4.8 %collective-permute-start.2 = (bf16[4,4,64,256]{3,2,1,0:T(8,128)(2,1)S(1)}, bf16[4,4,64,256]{3,2,1,0:T(8,128)(2,1)S(1)}, u32[]{:S(2)}, u32[]{:S(2)}) collective-permute-start(bf16[4,4,64,256]{3,2,1,0:T(8,128)(2,1)S(1)} %get-tuple-element.16.own1.refs_1_), channel_id=1, source_target_pairs={{0,32},{32,64},{64,96},{96,128},{128,160},{160,192},{192,224},{1,3... | collective-permute-start | bytes 1572872 | tf_op jit(solution)/shard_map/ppermute | solution.py:382
  15.4 0.6 collective-permute-start.4
  16.0 2.3 %collective-permute-done.4 = f32[8,128]{1,0:T(8,128)S(1)} collective-permute-done((f32[8,128]{1,0:T(8,128)S(1)}, f32[8,128]{1,0:T(8,128)S(1)}, u32[]{:S(2)}, u32[]{:S(2)}) %collective-permute-start.4) | collective-permute-done | bytes 4128 | tf_op jit(solution)/shard_map/ppermute | solution.py:392
  18.3 1.0 collective-permute-start.5
  19.2 3.1 %collective-permute-done.5 = f32[16,128]{1,0:T(8,128)S(1)} collective-permute-done((f32[16,128]{1,0:T(8,128)S(1)}, f32[16,128]{1,0:T(8,128)S(1)}, u32[]{:S(2)}, u32[]{:S(2)}) %collective-permute-start.5) | collective-permute-done | bytes 8224 | tf_op jit(solution)/shard_map/ppermute | solution.py:392
  22.3 0.0 collective-permute-done.zlow.refs_2_
  22.3 0.3 collective-permute-done.1.zhigh.refs_3_
  22.6 0.7 shard_map.75
  23.4 6.3 %collective-permute-start.6 = (bf16[2,4,64,256]{3,2,1,0:T(8,128)(2,1)}, bf16[2,4,64,256]{3,2,1,0:T(8,128)(2,1)S(1)}, u32[]{:S(2)}, u32[]{:S(2)}) collective-permute-start(bf16[2,4,64,256]{3,2,1,0:T(8,128)(2,1)} %get-tuple-element.20), channel_id=1, source_target_pairs={{0,32},{32,64},{64,96},{96,128},{128,160},{160,192},{192,224},{1,3... | collective-permute-start | bytes 786440 | tf_op jit(solution)/shard_map/ppermute | solution.py:382
  29.7 1.9 %collective-permute-start.7 = (bf16[2,4,64,256]{3,2,1,0:T(8,128)(2,1)S(1)}, bf16[2,4,64,256]{3,2,1,0:T(8,128)(2,1)S(1)}, u32[]{:S(2)}, u32[]{:S(2)}) collective-permute-start(bf16[2,4,64,256]{3,2,1,0:T(8,128)(2,1)S(1)} %get-tuple-element.21), channel_id=1, source_target_pairs={{32,0},{64,32},{96,64},{128,96},{160,128},{192,160},{224,192},{33,... | collective-permute-start | bytes 786440 | tf_op jit(solution)/shard_map/ppermute | solution.py:382
  31.6 11.8 %all-to-all-start = ((f32[64,1,128]{2,1,0:T(1,128)}), f32[64,1,128]{2,1,0:T(1,128)S(1)}, u32[]{:S(2)}, u32[]{:S(2)}) async-start(f32[64,1,128]{2,1,0:T(1,128)} %bitcast.1), calls=%async_computation | async-start | bytes 65536 | tf_op jit(solution)/shard_map/all_to_all | solution.py:399
  43.5 0.0 collective-permute-done.3.xhigh.refs_5_
  43.5 0.0 collective-permute-done.2.xlow.refs_4_
  43.5 0.0 copy-start.4
  43.5 0.0 copy-start.7
  43.5 0.0 copy-start.8
  43.5 1.2 %shard_map.76 = (bf16[4,6,64,256]{3,2,1,0:T(8,128)(2,1)}, bf16[4,6,64,256]{3,2,1,0:T(8,128)(2,1)}) custom-call(bf16[4,4,64,256]{3,2,1,0:T(8,128)(2,1)S(1)} %get-tuple-element.15.own0.refs_0_, bf16[4,4,64,256]{3,2,1,0:T(8,128)(2,1)S(1)} %get-tuple-element.16.own1.refs_1_, bf16[2,4,64,256]{3,2,1,0:T(8,128)(2,1)S(1)} %collective-permute-done.zlow.refs_2_, ...), custom_call_target="tpu_custom_call" | custom-call | tf_op jit(solution)/shard_map/pallas_call | solution.py:132
  44.8 1.3 %collective-permute-start.8 = (bf16[4,6,64,256]{3,2,1,0:T(8,128)(2,1)}, bf16[4,6,64,256]{3,2,1,0:T(8,128)(2,1)}, u32[]{:S(2)}, u32[]{:S(2)}) collective-permute-start(bf16[4,6,64,256]{3,2,1,0:T(8,128)(2,1)} %get-tuple-element.22), channel_id=1, source_target_pairs={{0,8},{8,16},{16,24},{1,9},{9,17},{17,25},{2,10},{10,18},{18,26},{... | collective-permute-start | bytes 2359304 | tf_op jit(solution)/shard_map/ppermute | solution.py:382
  46.1 0.0 copy-start.5
  46.1 4.9 %collective-permute-start.9 = (bf16[4,6,64,256]{3,2,1,0:T(8,128)(2,1)}, bf16[4,6,64,256]{3,2,1,0:T(8,128)(2,1)}, u32[]{:S(2)}, u32[]{:S(2)}) collective-permute-start(bf16[4,6,64,256]{3,2,1,0:T(8,128)(2,1)} %get-tuple-element.23), channel_id=1, source_target_pairs={{8,0},{16,8},{24,16},{9,1},{17,9},{25,17},{10,2},{18,10},{26,18},{... | collective-permute-start | bytes 2359304 | tf_op jit(solution)/shard_map/ppermute | solution.py:382
  51.0 1.6 %all-to-all-done = f32[64,1,128]{2,1,0:T(1,128)S(1)} async-done(((f32[64,1,128]{2,1,0:T(1,128)}), f32[64,1,128]{2,1,0:T(1,128)S(1)}, u32[]{:S(2)}, u32[]{:S(2)}) %all-to-all-start) | async-done | bytes 32800 | tf_op jit(solution)/shard_map/all_to_all | solution.py:399
  52.7 0.7 copy-done.6
  53.3 1.0 %copy-done.3 = bf16[256,768]{1,0:T(8,128)(2,1)S(1)} copy-done((bf16[256,768]{1,0:T(8,128)(2,1)S(1)}, bf16[256,768]{1,0:T(8,128)(2,1)}, u32[]{:S(2)}) %copy-start.3) | copy-done | bytes 393240
  54.3 18.4 %shard_map.77.refs_10_ = bf16[8,8,16,256]{3,2,1,0:T(8,128)(2,1)S(1)} custom-call(s32[2,4,4]{2,1,0:T(4,128)S(1)} %copy-done.5, bf16[4,4,64,256]{3,2,1,0:T(8,128)(2,1)S(1)} %get-tuple-element.15.own0.refs_0_, bf16[4,4,64,256]{3,2,1,0:T(8,128)(2,1)S(1)} %get-tuple-element.16.own1.refs_1_, bf16[2,4,64,256]{3,2,1,0:T(8,128)(2,1)S(1)} %collective-permute-done.zlow.refs_2_, ...), custom_call_target="tpu_custom_call" | custom-call | flops 15000000512 | bytes 8000000 | tf_op jit(solution)/shard_map/pallas_call | solution.py:353
  72.7 0.8 copy-done.9
  73.5 22.2 %shard_map.78 = bf16[8,16,16,256]{3,2,1,0:T(8,128)(2,1)} custom-call(s32[2,4,4]{2,1,0:T(4,128)S(1)} %copy-done.5, bf16[4,4,64,256]{3,2,1,0:T(8,128)(2,1)S(1)} %get-tuple-element.15.own0.refs_0_, bf16[4,4,64,256]{3,2,1,0:T(8,128)(2,1)S(1)} %get-tuple-element.16.own1.refs_1_, bf16[2,4,64,256]{3,2,1,0:T(8,128)(2,1)S(1)} %collective-permute-done.zlow.refs_2_, ...), custom_call_target="tpu_custom_call" | custom-call | flops 15000000512 | bytes 8000000 | tf_op jit(solution)/shard_map/pallas_call | solution.py:353
  (18 shorter events, 0.0 us)
Async XLA Ops:
  0.0 1.2 %copy-start = (bf16[8,16,16,256]{3,2,1,0:T(8,128)(2,1)S(1)}, bf16[8,16,16,256]{3,2,1,0:T(8,128)(2,1)}, u32[]{:S(2)}) copy-start(bf16[8,16,16,256]{3,2,1,0:T(8,128)(2,1)} %x_ref.3) | copy-start | bytes 3145732
  1.4 20.9 %collective-permute-start = (bf16[2,4,64,256]{3,2,1,0:T(8,128)(2,1)S(1)}, bf16[2,4,64,256]{3,2,1,0:T(8,128)(2,1)S(1)}, u32[]{:S(2)}, u32[]{:S(2)}) collective-permute-start(bf16[2,4,64,256]{3,2,1,0:T(8,128)(2,1)S(1)} %get-tuple-element.17), channel_id=1, source_target_pairs={{0,1},{1,2},{2,3},{3,4},{4,5},{5,6},{6,7},{8,9},{9,10},{10,11},{11... | collective-permute-start | bytes 786440 | tf_op jit(solution)/shard_map/ppermute | solution.py:382
  4.9 17.7 %collective-permute-start.1 = (bf16[2,4,64,256]{3,2,1,0:T(8,128)(2,1)S(1)}, bf16[2,4,64,256]{3,2,1,0:T(8,128)(2,1)S(1)}, u32[]{:S(2)}, u32[]{:S(2)}) collective-permute-start(bf16[2,4,64,256]{3,2,1,0:T(8,128)(2,1)S(1)} %get-tuple-element.18), channel_id=1, source_target_pairs={{1,0},{2,1},{3,2},{4,3},{5,4},{6,5},{7,6},{9,8},{10,9},{11,10},{12... | collective-permute-start | bytes 786440 | tf_op jit(solution)/shard_map/ppermute | solution.py:382
  7.8 35.7 %collective-permute-start.3 = (bf16[4,4,64,256]{3,2,1,0:T(8,128)(2,1)S(1)}, bf16[4,4,64,256]{3,2,1,0:T(8,128)(2,1)S(1)}, u32[]{:S(2)}, u32[]{:S(2)}) collective-permute-start(bf16[4,4,64,256]{3,2,1,0:T(8,128)(2,1)S(1)} %get-tuple-element.15.own0.refs_0_), channel_id=1, source_target_pairs={{32,0},{64,32},{96,64},{128,96},{160,128},{192,160},{224,192},{33,... | collective-permute-start | bytes 1572872 | tf_op jit(solution)/shard_map/ppermute | solution.py:382
  10.6 32.8 %collective-permute-start.2 = (bf16[4,4,64,256]{3,2,1,0:T(8,128)(2,1)S(1)}, bf16[4,4,64,256]{3,2,1,0:T(8,128)(2,1)S(1)}, u32[]{:S(2)}, u32[]{:S(2)}) collective-permute-start(bf16[4,4,64,256]{3,2,1,0:T(8,128)(2,1)S(1)} %get-tuple-element.16.own1.refs_1_), channel_id=1, source_target_pairs={{0,32},{32,64},{64,96},{96,128},{128,160},{160,192},{192,224},{1,3... | collective-permute-start | bytes 1572872 | tf_op jit(solution)/shard_map/ppermute | solution.py:382
  15.4 2.8 %collective-permute-start.4 = (f32[8,128]{1,0:T(8,128)S(1)}, f32[8,128]{1,0:T(8,128)S(1)}, u32[]{:S(2)}, u32[]{:S(2)}) collective-permute-start(f32[8,128]{1,0:T(8,128)S(1)} %get-tuple-element.19), channel_id=1, source_target_pairs={{0,8},{8,0},{16,24},{24,16},{1,9},{9,1},{17,25},{25,17},{2,10},{10... | collective-permute-start | bytes 12296 | tf_op jit(solution)/shard_map/ppermute | solution.py:392
  18.3 4.0 %collective-permute-start.5 = (f32[16,128]{1,0:T(8,128)S(1)}, f32[16,128]{1,0:T(8,128)S(1)}, u32[]{:S(2)}, u32[]{:S(2)}) collective-permute-start(f32[16,128]{1,0:T(8,128)S(1)} %pad_maximum_fusion.1), channel_id=1, source_target_pairs={{0,16},{8,24},{16,0},{24,8},{1,17},{9,25},{17,1},{25,9},{2,18},{10... | collective-permute-start | bytes 24584 | tf_op jit(solution)/shard_map/ppermute | solution.py:392
  23.4 20.1 %collective-permute-start.6 = (bf16[2,4,64,256]{3,2,1,0:T(8,128)(2,1)}, bf16[2,4,64,256]{3,2,1,0:T(8,128)(2,1)S(1)}, u32[]{:S(2)}, u32[]{:S(2)}) collective-permute-start(bf16[2,4,64,256]{3,2,1,0:T(8,128)(2,1)} %get-tuple-element.20), channel_id=1, source_target_pairs={{0,32},{32,64},{64,96},{96,128},{128,160},{160,192},{192,224},{1,3... | collective-permute-start | bytes 786440 | tf_op jit(solution)/shard_map/ppermute | solution.py:382
  29.7 13.8 %collective-permute-start.7 = (bf16[2,4,64,256]{3,2,1,0:T(8,128)(2,1)S(1)}, bf16[2,4,64,256]{3,2,1,0:T(8,128)(2,1)S(1)}, u32[]{:S(2)}, u32[]{:S(2)}) collective-permute-start(bf16[2,4,64,256]{3,2,1,0:T(8,128)(2,1)S(1)} %get-tuple-element.21), channel_id=1, source_target_pairs={{32,0},{64,32},{96,64},{128,96},{160,128},{192,160},{224,192},{33,... | collective-permute-start | bytes 786440 | tf_op jit(solution)/shard_map/ppermute | solution.py:382
  31.6 21.0 %all-to-all-start = ((f32[64,1,128]{2,1,0:T(1,128)}), f32[64,1,128]{2,1,0:T(1,128)S(1)}, u32[]{:S(2)}, u32[]{:S(2)}) async-start(f32[64,1,128]{2,1,0:T(1,128)} %bitcast.1), calls=%async_computation | async-start | bytes 65536 | tf_op jit(solution)/shard_map/all_to_all | solution.py:399
  43.5 1.3 %copy-start.1 = (bf16[4,4,64,256]{3,2,1,0:T(8,128)(2,1)}, bf16[4,4,64,256]{3,2,1,0:T(8,128)(2,1)S(1)}, u32[]{:S(2)}) copy-start(bf16[4,4,64,256]{3,2,1,0:T(8,128)(2,1)S(1)} %collective-permute-done.3.xhigh.refs_5_) | copy-start | bytes 1572868
  43.5 9.2 %copy-start.4 = (bf16[256,256]{1,0:T(8,128)(2,1)S(1)}, bf16[256,256]{1,0:T(8,128)(2,1)}, u32[]{:S(2)}) copy-start(bf16[256,256]{1,0:T(8,128)(2,1)} %refs_15_.1) | copy-start | bytes 393220
  43.5 9.1 %copy-start.7 = (f32[256]{0:T(256)S(1)}, f32[256]{0:T(256)}, u32[]{:S(2)}) copy-start(f32[256]{0:T(256)} %param.9) | copy-start | bytes 3076
  43.5 9.1 %copy-start.8 = (f32[256]{0:T(256)S(1)}, f32[256]{0:T(256)}, u32[]{:S(2)}) copy-start(f32[256]{0:T(256)} %param.12) | copy-start | bytes 3076
  44.8 28.7 %collective-permute-start.8 = (bf16[4,6,64,256]{3,2,1,0:T(8,128)(2,1)}, bf16[4,6,64,256]{3,2,1,0:T(8,128)(2,1)}, u32[]{:S(2)}, u32[]{:S(2)}) collective-permute-start(bf16[4,6,64,256]{3,2,1,0:T(8,128)(2,1)} %get-tuple-element.22), channel_id=1, source_target_pairs={{0,8},{8,16},{16,24},{1,9},{9,17},{17,25},{2,10},{10,18},{18,26},{... | collective-permute-start | bytes 2359304 | tf_op jit(solution)/shard_map/ppermute | solution.py:382
  46.1 6.6 %copy-start.5 = (s32[2,4,4]{2,1,0:T(4,128)S(1)}, s32[2,4,4]{2,1,0:T(4,128)}, u32[]{:S(2)}) copy-start(s32[2,4,4]{2,1,0:T(4,128)} %limit.3) | copy-start | bytes 388
  46.1 27.4 %collective-permute-start.9 = (bf16[4,6,64,256]{3,2,1,0:T(8,128)(2,1)}, bf16[4,6,64,256]{3,2,1,0:T(8,128)(2,1)}, u32[]{:S(2)}, u32[]{:S(2)}) collective-permute-start(bf16[4,6,64,256]{3,2,1,0:T(8,128)(2,1)} %get-tuple-element.23), channel_id=1, source_target_pairs={{8,0},{16,8},{24,16},{9,1},{17,9},{25,17},{10,2},{18,10},{26,18},{... | collective-permute-start | bytes 2359304 | tf_op jit(solution)/shard_map/ppermute | solution.py:382
  52.7 0.7 copy-start.6
  53.3 1.0 %copy-start.3 = (bf16[256,768]{1,0:T(8,128)(2,1)S(1)}, bf16[256,768]{1,0:T(8,128)(2,1)}, u32[]{:S(2)}) copy-start(bf16[256,768]{1,0:T(8,128)(2,1)} %refs_14_.1) | copy-start | bytes 1179652
  54.3 19.2 %copy-start.2 = (bf16[4,4,64,256]{3,2,1,0:T(8,128)(2,1)S(1)}, bf16[4,4,64,256]{3,2,1,0:T(8,128)(2,1)}, u32[]{:S(2)}) copy-start(bf16[4,4,64,256]{3,2,1,0:T(8,128)(2,1)} %copy-done.1) | copy-start | bytes 1572868
  72.7 0.8 copy-start.9
